TPU v7x, 256 devices: a whole 4x4x8 slice. The times are simulated.
256 devices in a mesh: row: 32 (over x, y, core), col: 8 (over z).
Axes of the slice: x: 4, y: 4, z: 8, core: 2. Of those that a mesh axis runs over, the one named last changes fastest.
Arguments:
- features: bfloat16 [65536, 256], P(('row', 'col')), may hold values from -6 to 6
- weight_one: bfloat16 [256, 256], replicated, may hold values from -0.375 to 0.375
- weight_two: bfloat16 [256, 172], replicated, may hold values from -0.375 to 0.375
- adj_tiles: bfloat16 [32, 8, 128, 128, 128], P('row', 'col'), may hold values from -0.109375 to 0.109375
- tile_rows: int32 [32, 8, 128], P('row', 'col'), may hold values from 0 to 15
- tile_cols: int32 [32, 8, 128], P('row', 'col'), may hold values from 0 to 63
- tile_counts: int32 [32, 8], P('row', 'col'), may hold values from 32 to 128, as said below
- labels: int32 [65536], P('row'), may hold values from 0 to 171
Outputs:
- logits: float32 [65536, 172], P(('row', 'col'))
- grad_one: float32 [256, 256], replicated
- grad_two: float32 [256, 172], replicated
Inputs may be any that keep to these rules, and one draw needn't show every extreme that they name: `tile_counts`: one device has all 128 slots live.
All inputs are finite; a program needn't handle non-finite values.
Results may differ from a plain program's by a relative error of at most 0.007.
Values may be sent and summed in bfloat16 or wider, within the bound.
No kernel may reach another device: no remote copies, remote signals or barrier semaphores. Data moves between devices by JAX's collectives and lax.ppermute only.
A program may use at most 64 MiB of HBM per device.

v0:
```python
import math

import jax
import jax.numpy as jnp
from jax import lax
from jax.sharding import PartitionSpec as P


def aggregate(tile_block, row_ids, col_ids, tile_count, source, out_blocks, transposed):
    tile_size = tile_block.shape[1]
    feat_width = source.shape[-1]
    stacked = source.reshape(-1, tile_size, feat_width)
    group_len = math.gcd(32, tile_block.shape[0])

    def one_group(group_index, running):
        first_slot = group_index * group_len
        tile_piece = lax.dynamic_slice_in_dim(tile_block, first_slot, group_len, 0)
        row_piece = lax.dynamic_slice_in_dim(row_ids, first_slot, group_len, 0)
        col_piece = lax.dynamic_slice_in_dim(col_ids, first_slot, group_len, 0)
        live_mask = (first_slot + jnp.arange(group_len, dtype=jnp.int32) < tile_count).astype(
            jnp.float32
        )
        if transposed:
            picked = stacked[row_piece]
            product = jnp.einsum(
                "gji,gjw->giw", tile_piece, picked, preferred_element_type=jnp.float32
            )
            target = col_piece
        else:
            picked = stacked[col_piece]
            product = jnp.einsum(
                "gij,gjw->giw", tile_piece, picked, preferred_element_type=jnp.float32
            )
            target = row_piece
        return running.at[target].add(product * live_mask[:, None, None])

    last_group = tile_block.shape[0] // group_len
    running = jnp.zeros((out_blocks, tile_size, feat_width), jnp.float32)
    running = lax.fori_loop(0, last_group, one_group, running)
    return running.reshape(out_blocks * tile_size, feat_width)


def loss_grad(logit_block, label_block, node_total):
    softened = jax.nn.softmax(logit_block, axis=-1)
    class_ids = jnp.arange(logit_block.shape[1], dtype=jnp.int32)
    onehot = (label_block[:, None] == class_ids[None, :]).astype(jnp.float32)
    return ((softened - onehot) * node_total ** (-0.5)).astype(jnp.bfloat16)


def body(features, weight_one, weight_two, adj_tiles, tile_rows, tile_cols, tile_counts, labels):
    tile_block = adj_tiles[0, 0]
    row_ids = tile_rows[0, 0]
    col_ids = tile_cols[0, 0]
    tile_count = tile_counts[0, 0]
    rows_dev = features.shape[0]
    tile_size = tile_block.shape[1]
    row_devices = lax.axis_size("row")
    col_devices = lax.axis_size("col")
    group_blocks = col_devices * rows_dev // tile_size
    panel_blocks = row_devices * rows_dev // tile_size
    node_total = row_devices * col_devices * rows_dev
    row_panel = lax.all_gather(features, "row", axis=0, tiled=True)
    partial_one = aggregate(
        tile_block, row_ids, col_ids, tile_count, row_panel, group_blocks, False
    )
    aggregated = lax.psum_scatter(partial_one, "col", scatter_dimension=0, tiled=True).astype(
        jnp.bfloat16
    )
    hidden_pre = jnp.dot(aggregated, weight_one, preferred_element_type=jnp.float32)
    hidden = jax.nn.silu(hidden_pre).astype(jnp.bfloat16)
    projected = jnp.dot(hidden, weight_two, preferred_element_type=jnp.float32).astype(jnp.bfloat16)
    projected_panel = lax.all_gather(projected, "row", axis=0, tiled=True)
    partial_two = aggregate(
        tile_block, row_ids, col_ids, tile_count, projected_panel, group_blocks, False
    )
    own_start = lax.axis_index("col") * rows_dev
    logits = lax.psum_scatter(partial_two, "col", scatter_dimension=0, tiled=True)
    own_labels = lax.dynamic_slice_in_dim(labels, own_start, rows_dev, 0)
    group_grad = lax.all_gather(
        loss_grad(logits, own_labels, node_total), "col", axis=0, tiled=True
    )
    partial_back = aggregate(
        tile_block, row_ids, col_ids, tile_count, group_grad, panel_blocks, True
    )
    back_grad = lax.psum_scatter(partial_back, "row", scatter_dimension=0, tiled=True).astype(
        jnp.bfloat16
    )
    grad_two = jnp.einsum("nh,nc->hc", hidden, back_grad, preferred_element_type=jnp.float32)
    grad_two = lax.psum(grad_two, ("row", "col"))
    hidden_grad = jnp.einsum("nc,hc->nh", back_grad, weight_two, preferred_element_type=jnp.float32)
    gate_value = jax.nn.sigmoid(hidden_pre)
    derivative = gate_value * (1.0 + hidden_pre * (1.0 - gate_value))
    pre_grad = (hidden_grad * derivative).astype(jnp.bfloat16)
    grad_one = jnp.einsum("nf,nh->fh", aggregated, pre_grad, preferred_element_type=jnp.float32)
    grad_one = lax.psum(grad_one, ("row", "col"))
    return (logits, grad_one, grad_two)


def solution(mesh):
    in_specs = (
        P(("row", "col"), None),
        P(),
        P(),
        P("row", "col", None, None, None),
        P("row", "col", None),
        P("row", "col", None),
        P("row", "col"),
        P("row"),
    )
    out_specs = (P(("row", "col"), None), P(), P())
    return jax.shard_map(body, mesh=mesh, in_specs=in_specs, out_specs=out_specs, check_vma=False)
```

profile of v0, /device:TPU:1, one launch (start us, length us, event | category | flops | bytes accessed | tf_op | source)
XLA Modules:
  0.0 798.2 jit_solution(15496289920186886055)
XLA Ops:
  8.0 57.9 %all-gather.3.cloned.1.call-done = bf16[8192,256]{1,0:T(8,128)(2,1)} async-done(((bf16[256,256]{1,0:T(8,128)(2,1)}), bf16[8192,256]{1,0:T(8,128)(2,1)}) %all-gather.3.cloned.1.call-update) | async-done | bytes 4194320 | tf_op jit(solution)/shard_map/all_gather | solution.py:62
  66.1 67.0 %while.39 = (s32[]{:T(128)}, f32[16,128,256]{2,1,0:T(8,128)S(1)}, s32[128]{0:T(128)}, bf16[128,128,128]{2,1,0:T(8,128)(2,1)}, s32[128]{0:T(128)}, /*index=5*/bf1...) while((s32[]{:T(128)}, f32[16,128,256]{2,1,0:T(8,128)S(1)}, ...), condition=%wide.region_2.0_spmd, body=%wide.region_0.0_spmd.sunk | while | flops 270533920 | bytes 24122668 | solution.py:39
  67.6 4.2 gather_fusion
  71.8 4.6 convolution_multiply_fusion.7
  76.4 6.5 scatter_fusion
  84.3 4.2 gather_fusion
  88.6 4.6 convolution_multiply_fusion.7
  93.2 6.5 scatter_fusion
  101.1 4.2 gather_fusion
  105.3 4.6 convolution_multiply_fusion.7
  109.9 6.5 scatter_fusion
  117.8 4.2 gather_fusion
  122.1 4.6 convolution_multiply_fusion.7
  126.7 6.5 scatter_fusion
  134.6 37.1 %reduce-scatter.4.cloned.1.call-done = f32[256,256]{1,0:T(8,128)} async-done(((f32[2048,256]{1,0:T(8,128)}), f32[256,256]{1,0:T(8,128)}) %reduce-scatter.4.cloned.1.call-update) | async-done | bytes 262160 | tf_op jit(solution)/shard_map/reduce_scatter | solution.py:66
  173.8 55.6 %all-gather.5.cloned.1.call-done = bf16[8192,172]{0,1:T(8,128)(2,1)} async-done(((bf16[256,172]{0,1:T(8,128)(2,1)}), bf16[8192,172]{0,1:T(8,128)(2,1)}) %all-gather.5.cloned.1.call-update) | async-done | bytes 2818064 | tf_op jit(solution)/shard_map/all_gather | solution.py:72
  229.4 5.8 copy.24
  236.4 58.5 %while.40 = (s32[]{:T(128)}, f32[16,128,172]{1,2,0:T(8,128)}, s32[128]{0:T(128)S(1)}, bf16[128,128,128]{2,1,0:T(8,128)(2,1)}, s32[128]{0:T(128)S(1)}, /*index=5*...) while((s32[]{:T(128)}, f32[16,128,172]{1,2,0:T(8,128)}, ...), condition=%wide.region_6.7_spmd, body=%wide.region_4.6_spmd.sunk | while | flops 181765408 | bytes 17241388 | solution.py:39
  237.1 4.2 gather_fusion.1
  241.3 2.8 convolution_multiply_fusion.8
  244.1 7.0 scatter_fusion.1
  251.8 4.2 gather_fusion.1
  256.0 2.8 convolution_multiply_fusion.8
  258.8 6.9 scatter_fusion.1
  266.4 4.2 gather_fusion.1
  273.4 6.9 scatter_fusion.1
  281.0 4.2 gather_fusion.1
  288.0 6.9 scatter_fusion.1
  299.3 34.5 %reduce-scatter.6.cloned.1.call-done = f32[256,172]{0,1:T(8,128)} async-done(((f32[2048,172]{0,1:T(8,128)}), f32[256,172]{0,1:T(8,128)}) %reduce-scatter.6.cloned.1.call-update) | async-done | bytes 176144 | tf_op jit(solution)/shard_map/reduce_scatter | solution.py:77
  336.7 20.4 %all_gather.11 = bf16[2048,172]{0,1:T(8,128)(2,1)S(1)} all-gather(bf16[256,172]{0,1:T(8,128)(2,1)S(1)} %multiply_convert_fusion.1), channel_id=1, replica_groups=mesh['row'=32,'col'=8] {'col'}, dimensions={0}, use_global_device_ids=true | all-gather | bytes 792576 | tf_op jit(solution)/shard_map/all_gather | solution.py:79
  358.5 2.9 broadcast_in_dim.66
  361.4 55.6 %while.41 = (s32[]{:T(128)}, f32[64,128,172]{1,2,0:T(8,128)}, s32[128]{0:T(128)S(1)}, bf16[128,128,128]{2,1,0:T(8,128)(2,1)}, s32[128]{0:T(128)S(1)}, /*index=5*...) while((s32[]{:T(128)}, f32[64,128,172]{1,2,0:T(8,128)}, ...), condition=%wide.region_12.13_spmd, body=%wide.region_10.12_spmd.sunk | while | flops 181765408 | bytes 17241388 | solution.py:39
  362.1 3.2 gather_fusion.2
  365.3 2.8 convolution_multiply_fusion.9
  368.1 7.2 scatter_fusion.2
  376.0 3.2 gather_fusion.2
  379.3 2.8 convolution_multiply_fusion.9
  382.1 7.2 scatter_fusion.2
  390.0 3.2 gather_fusion.2
  393.3 2.8 convolution_multiply_fusion.9
  396.1 7.1 scatter_fusion.2
  403.9 3.2 gather_fusion.2
  407.1 2.8 convolution_multiply_fusion.9
  409.9 7.0 scatter_fusion.2
  416.9 4.4 copy.30
  422.4 7.4 copy.27
  429.8 100.1 %reduce-scatter.8.cloned.1.call-done = f32[256,172]{0,1:T(8,128)} async-done(((f32[8192,172]{0,1:T(8,128)}), f32[256,172]{0,1:T(8,128)}) %reduce-scatter.8.cloned.1.call-update) | async-done | bytes 176144 | tf_op jit(solution)/shard_map/reduce_scatter | solution.py:85
  533.8 254.3 %all-reduce.3.cloned.1.call-done = (f32[256,256]{1,0:T(8,128)}, f32[256,172]{0,1:T(8,128)}) async-done(((f32[256,256]{1,0:T(8,128)}, f32[256,172]{0,1:T(8,128)}), (f32[256,256]{1,0:T(8,128)}, f32[256,172]{0,1:T(8,128)})) %all-reduce.3.cloned.1.call-update) | async-done | bytes 438288 | tf_op jit(solution)/shard_map/psum | solution.py:95
  (79 shorter events, 39.5 us)
Async XLA Ops:
  7.2 164.5 %copy-start = (bf16[256,256]{1,0:T(8,128)(2,1)S(1)}, bf16[256,256]{1,0:T(8,128)(2,1)}, u32[]{:S(2)}) copy-start(bf16[256,256]{1,0:T(8,128)(2,1)} %param.15) | copy-start | bytes 393220
  7.2 58.7 %all-gather.3.cloned.1.call-start = ((), (), s32[]{:S(2)}) async-start(), calls=%async_computation.3 | async-start | bytes 4325376 | tf_op jit(solution)/shard_map/all_gather | solution.py:62
  7.9 163.8 %reduce-scatter.4.cloned.1.call-start = ((), (), s32[]{:S(2)}) async-start(), calls=%async_computation.4 | async-start | bytes 2359296 | tf_op jit(solution)/shard_map/reduce_scatter | solution.py:66
  66.1 106.7 %copy-start.5 = (bf16[256,172]{0,1:T(8,128)(2,1)S(1)}, bf16[256,172]{0,1:T(8,128)(2,1)}, u32[]{:S(2)}) copy-start(bf16[256,172]{0,1:T(8,128)(2,1)} %param.16) | copy-start | bytes 264196
  133.2 1.3 copy-start.1
  134.5 94.9 %all-gather.5.cloned.1.call-start = ((), (), s32[]{:S(2)}) async-start(), calls=%async_computation.5 | async-start | bytes 2973696 | tf_op jit(solution)/shard_map/all_gather | solution.py:72
  173.7 160.1 %reduce-scatter.6.cloned.1.call-start = ((), (), s32[]{:S(2)}) async-start(), calls=%async_computation.6 | async-start | bytes 1622016 | tf_op jit(solution)/shard_map/reduce_scatter | solution.py:77
  173.8 62.6 %copy-start.3 = (s32[128]{0:T(128)S(1)}, s32[128]{0:T(128)}, u32[]{:S(2)}) copy-start(s32[128]{0:T(128)} %get-tuple-element.728) | copy-start | bytes 1540
  173.8 62.6 %copy-start.4 = (s32[128]{0:T(128)S(1)}, s32[128]{0:T(128)}, u32[]{:S(2)}) copy-start(s32[128]{0:T(128)} %get-tuple-element.730) | copy-start | bytes 1540
  298.5 231.4 %reduce-scatter.8.cloned.1.call-start = ((), (), s32[]{:S(2)}) async-start(), calls=%async_computation.7 | async-start | bytes 5947392 | tf_op jit(solution)/shard_map/reduce_scatter | solution.py:85
  429.8 100.2 %copy-start.2 = (f32[256,256]{1,0:T(8,128)S(1)}, f32[256,256]{1,0:T(8,128)}, u32[]{:S(2)}) copy-start(f32[256,256]{1,0:T(8,128)} %reduce-scatter.4.cloned.1.call-done) | copy-start | bytes 786436
  429.8 358.3 %all-reduce.3.cloned.1.call-start = ((), (), s32[]{:S(2)}) async-start(), calls=%async_computation.8 | async-start | bytes 884736 | tf_op jit(solution)/shard_map/psum | solution.py:95
Sparse Core Ops, SparseCore 0:
  10.6 55.2 all-gather.2
  134.6 36.9 reduce-scatter.3
  174.7 54.6 all-gather.4
  298.6 35.1 reduce-scatter.5
  429.9 99.9 reduce-scatter.7
  536.9 251.1 all-reduce.2
where the time goes:
time: 800 us; the launch traced here: 798 us
  waiting for transfers between devices  540 us (68%)
  other arithmetic  96.6 us (12%)
  local copies, waits for them, and re-layouts  79.7 us (10%)
  matrix products  46.5 us (6%)
  blocking collectives  20.4 us (3%)
  between operations  14.2 us (2%)
    psum x1, waiting for transfers between devices, body(): grad_one = lax.psum(grad_one, ('row', 'col'))  254 us
    reduce_scatter x1, waiting for transfers between devices, body(): lax.psum_scatter(partial_back, 'row', scatter_dimension=0, tiled=True)  100 us
    scatter-add x12, other arithmetic, one_group(): return running.at[target].add(product * live_mask[:, None, None])  82.2 us
    all_gather x1, waiting for transfers between devices, body(): row_panel = lax.all_gather(features, 'row', axis=0, tiled=True)  57.9 us
    all_gather x1, waiting for transfers between devices, body(): projected_panel = lax.all_gather(projected, 'row', axis=0, tiled=True)  55.6 us
    reduce_scatter x1, waiting for transfers between devices, body(): lax.psum_scatter(partial_one, 'col', scatter_dimension=0, tiled=True)  37.1 us
    reduce_scatter x1, waiting for transfers between devices, body(): lax.psum_scatter(partial_two, 'col', scatter_dimension=0, tiled=True)  34.5 us
    gather x8, local copies, waits for them, and re-layouts, one_group(): picked = stacked[col_piece]  33.7 us
  transfers between devices with their start and end apart: 6, of which 6 were waited for; matrix products, arithmetic and copies ran while one was open for 0% of the time, Pallas kernels for 0%

commit v1 on v0

v1 whole, which is shorter than its diff:
```python
import functools

import jax
import jax.numpy as jnp
from jax import lax
from jax.experimental import pallas as pl
from jax.experimental.pallas import tpu as pltpu
from jax.sharding import PartitionSpec as P

F32 = jnp.float32
BF16 = jnp.bfloat16
NT = (((1,), (1,)), ((), ()))
NN = (((1,), (0,)), ((), ()))
TB = 128
GX, GY, GZ = 4, 4, 8
ROWS = 256
FEAT = 256
CLASSES = 172
CPAD = 176
SLOTS = 128
FWD = 4
BWD = 2
FWD_GROUPS = 48
BWD_GROUPS = 98
VMEM_LIMIT = 56 * 1024 * 1024


def params():
    return pltpu.CompilerParams(vmem_limit_bytes=VMEM_LIMIT)


def any_spec():
    return pl.BlockSpec(memory_space=pl.ANY)


def vmem_spec():
    return pl.BlockSpec(memory_space=pltpu.VMEM)


def smem_spec():
    return pl.BlockSpec(memory_space=pltpu.SMEM)


def row_perm(move):
    pairs = []
    for index in range(GX * GY * 2):
        x, y, core = index // (2 * GY), (index // 2) % GY, index % 2
        x, y, core = move(x, y, core)
        pairs.append((index, ((x % GX) * GY + y % GY) * 2 + core))
    return pairs


def first_axis(step):
    return row_perm(lambda x, y, c: (x, y + step, c) if c == 0 else (x + step, y, c))


def second_axis(step):
    return row_perm(lambda x, y, c: (x + step, y, c) if c == 0 else (x, y + step, c))


def swap_core():
    return row_perm(lambda x, y, c: (x, y, 1 - c))


def gather_row(own):
    send = lambda v, perm: lax.ppermute(v, "row", perm)
    line = jnp.concatenate(
        [
            own,
            send(own, first_axis(-1)),
            send(own, first_axis(2)),
            send(own, first_axis(1)),
        ],
        0,
    )
    line_swap = send(line, swap_core())
    half = line.shape[0] // 2
    plus = send(line, second_axis(-1))
    minus = send(line, second_axis(1))
    two_low = send(line[:half], second_axis(2))
    two_high = send(plus[half:], second_axis(-1))
    two = jnp.concatenate([two_low, two_high], 0)
    return [
        line,
        plus,
        two,
        minus,
        line_swap,
        send(plus, swap_core()),
        send(two, swap_core()),
        send(minus, swap_core()),
    ]


def source_slots(col_ids):
    me = lax.axis_index("row")
    x, y, core = me // (2 * GY), (me // 2) % GY, me % 2
    device = col_ids // 2
    dx = (device // (2 * GY) - x) % GX
    dy = ((device // 2) % GY - y) % GY
    other = device % 2
    along_first = jnp.where(other == 0, dy, dx)
    along_second = jnp.where(other == 0, dx, dy)
    far = (other != core).astype(jnp.int32)
    return ((far * 4 + along_second) * 4 + along_first) * 2 + col_ids % 2


def gather_col(own):
    send = lambda v, step: lax.ppermute(v, "col", [(i, (i + step) % GZ) for i in range(GZ)])
    found = {0: own}
    up = down = own
    for step in range(1, 4):
        up, down = send(up, -1), send(down, 1)
        found[step], found[GZ - step] = up, down
    found[4] = send(up, -1)
    return [found[d] for d in range(GZ)]


def group_tiles(target, source, count, n_targets, group, n_groups):
    slots = jnp.arange(SLOTS, dtype=jnp.int32)
    live = slots < count
    key = jnp.where(live, target, n_targets)
    targets = jnp.arange(n_targets, dtype=jnp.int32)
    members = jnp.sum((key[None, :] == targets[:, None]).astype(jnp.int32), 1)
    groups = (members + group - 1) // group
    earlier = jnp.sum(
        jnp.where(targets[None, :] < key[:, None], groups[None, :], 0), 1
    )
    rank = jnp.sum(
        ((key[None, :] == key[:, None]) & (slots[None, :] < slots[:, None])).astype(jnp.int32), 1
    )
    place = jnp.where(live, earlier * group + rank, -1)
    places = jnp.arange(n_groups * group, dtype=jnp.int32)
    hit = place[None, :] == places[:, None]
    order = SLOTS + jnp.sum(jnp.where(hit, slots[None, :] - SLOTS, 0), 1)
    picked = jnp.sum(jnp.where(hit, source[None, :], 0), 1)
    goal = jnp.sum(jnp.where(hit, target[None, :], 0), 1)[::group]
    return jnp.concatenate([order, picked, goal, jnp.sum(groups)[None]]).astype(jnp.int32)


def load_tiles(tiles_hbm, tiles, sem):
    copy = pltpu.make_async_copy(tiles_hbm, tiles.at[pl.ds(0, SLOTS)], sem)
    copy.start()
    tiles[SLOTS] = jnp.zeros((TB, TB), BF16)
    return copy


def aggregate_kernel(table, tiles_hbm, *rest):
    pieces, (out, tiles, source, total, sems) = rest[:8], rest[8:]
    copies = [load_tiles(tiles_hbm, tiles, sems.at[0])]
    for index, piece in enumerate(pieces):
        copy = pltpu.make_async_copy(piece, source.at[pl.ds(index * 8, 8)], sems.at[index + 1])
        copy.start()
        copies.append(copy)
    total[...] = jnp.zeros_like(total)
    for copy in copies:
        copy.wait()
    width = FWD_GROUPS * FWD

    def product(g):
        left, right = [], []
        for k in range(FWD):
            left.append(tiles[table[g * FWD + k]])
            right.append(source[table[width + g * FWD + k]])
        return lax.dot_general(
            jnp.concatenate(left, 1),
            jnp.concatenate(right, 0),
            NN,
            preferred_element_type=F32,
        )

    def step(i, carry):
        first, second = product(2 * i), product(2 * i + 1)
        total[table[2 * width + 2 * i]] += first
        total[table[2 * width + 2 * i + 1]] += second
        return carry

    lax.fori_loop(0, (table[2 * width + FWD_GROUPS] + 1) // 2, step, 0)
    for d in range(GZ):
        out[d, 0:TB] = total[2 * d].astype(BF16)
        out[d, TB : 2 * TB] = total[2 * d + 1].astype(BF16)


def aggregate(table, tiles, pieces):
    return pl.pallas_call(
        aggregate_kernel,
        name="aggregate",
        out_shape=jax.ShapeDtypeStruct((GZ, ROWS, FEAT), BF16),
        in_specs=[smem_spec()] + [any_spec()] * 9,
        out_specs=vmem_spec(),
        scratch_shapes=[
            pltpu.VMEM((SLOTS + 1, TB, TB), BF16),
            pltpu.VMEM((64, TB, FEAT), BF16),
            pltpu.VMEM((16, TB, FEAT), F32),
            pltpu.SemaphoreType.DMA((9,)),
        ],
        compiler_params=params(),
        cost_estimate=pl.CostEstimate(flops=2 * 10**9, bytes_accessed=10**7, transcendentals=0),
    )(table, tiles, *[p.reshape(8, TB, FEAT) for p in pieces])


def middle_kernel(parts, weight_one, weight_two_t, agg, projected_t):
    summed = parts[0].astype(F32)
    for d in range(1, GZ):
        summed += parts[d].astype(F32)
    rounded = summed.astype(BF16)
    agg[...] = rounded
    pre = lax.dot_general(rounded, weight_one[...], NN, preferred_element_type=F32)
    hidden = (pre * jax.nn.sigmoid(pre)).astype(BF16)
    projected_t[...] = lax.dot_general(
        weight_two_t[...], hidden, NT, preferred_element_type=F32
    ).astype(BF16)


def middle(parts, weight_one, weight_two_t):
    return pl.pallas_call(
        middle_kernel,
        name="middle",
        out_shape=(
            jax.ShapeDtypeStruct((ROWS, FEAT), BF16),
            jax.ShapeDtypeStruct((CPAD, ROWS), BF16),
        ),
        in_specs=[vmem_spec()] * 3,
        out_specs=[vmem_spec()] * 2,
        compiler_params=params(),
    )(parts, weight_one, weight_two_t)


def logits_kernel(table, tiles_hbm, *rest):
    pieces, (out, tiles, source, total, sems) = rest[:8], rest[8:]
    copies = [load_tiles(tiles_hbm, tiles, sems.at[0])]
    for index, piece in enumerate(pieces):
        for block in range(4):
            for half in range(2):
                copy = pltpu.make_async_copy(
                    piece.at[block, :, pl.ds(half * TB, TB)],
                    source.at[(index * 4 + block) * 2 + half],
                    sems.at[index + 1],
                )
                copy.start()
                copies.append(copy)
    total[...] = jnp.zeros_like(total)
    for copy in copies:
        copy.wait()
    width = FWD_GROUPS * FWD

    def product(g):
        left, right = [], []
        for k in range(FWD):
            left.append(source[table[width + g * FWD + k]])
            right.append(tiles[table[g * FWD + k]])
        return lax.dot_general(
            jnp.concatenate(left, 1),
            jnp.concatenate(right, 1),
            NT,
            preferred_element_type=F32,
        )

    def step(i, carry):
        first, second = product(2 * i), product(2 * i + 1)
        total[table[2 * width + 2 * i]] += first
        total[table[2 * width + 2 * i + 1]] += second
        return carry

    lax.fori_loop(0, (table[2 * width + FWD_GROUPS] + 1) // 2, step, 0)
    for d in range(GZ):
        out[d, :, 0:TB] = total[2 * d].astype(BF16)
        out[d, :, TB : 2 * TB] = total[2 * d + 1].astype(BF16)


def partial_logits(table, tiles, pieces):
    return pl.pallas_call(
        logits_kernel,
        name="partial_logits",
        out_shape=jax.ShapeDtypeStruct((GZ, CPAD, ROWS), BF16),
        in_specs=[smem_spec()] + [any_spec()] * 9,
        out_specs=vmem_spec(),
        scratch_shapes=[
            pltpu.VMEM((SLOTS + 1, TB, TB), BF16),
            pltpu.VMEM((64, CPAD, TB), BF16),
            pltpu.VMEM((16, CPAD, TB), F32),
            pltpu.SemaphoreType.DMA((9,)),
        ],
        compiler_params=params(),
        cost_estimate=pl.CostEstimate(flops=2 * 10**9, bytes_accessed=10**7, transcendentals=0),
    )(table, tiles, *[p.reshape(4, CPAD, ROWS) for p in pieces])


def loss_kernel(scale, parts, labels, logits, grad_t):
    summed = parts[0].astype(F32)
    for d in range(1, GZ):
        summed += parts[d].astype(F32)
    logits[...] = jnp.transpose(summed)[:, :CLASSES]
    ids = lax.broadcasted_iota(jnp.int32, summed.shape, 0)
    valid = ids < CLASSES
    top = jnp.max(jnp.where(valid, summed, -jnp.inf), 0, keepdims=True)
    grown = jnp.where(valid, jnp.exp(summed - top), 0.0)
    soft = grown / jnp.sum(grown, 0, keepdims=True)
    onehot = (ids == labels[...]).astype(F32)
    grad_t[...] = ((soft - onehot) * scale).astype(BF16)


def loss_grad(parts, labels, scale):
    return pl.pallas_call(
        functools.partial(loss_kernel, scale),
        name="loss_grad",
        out_shape=(
            jax.ShapeDtypeStruct((ROWS, CLASSES), F32),
            jax.ShapeDtypeStruct((CPAD, ROWS), BF16),
        ),
        in_specs=[vmem_spec()] * 2,
        out_specs=[vmem_spec()] * 2,
        compiler_params=params(),
    )(parts, labels)


def gates_kernel(agg, weight_one_t, hidden_t, slope_t):
    pre = lax.dot_general(weight_one_t[...], agg[...], NT, preferred_element_type=F32)
    gate = jax.nn.sigmoid(pre)
    hidden_t[...] = (pre * gate).astype(BF16)
    slope_t[...] = (gate * (1.0 + pre * (1.0 - gate))).astype(BF16)


def gates(agg_panel, weight_one_t):
    nodes = agg_panel.shape[0]
    chunk = 1024
    return pl.pallas_call(
        gates_kernel,
        name="gates",
        grid=(nodes // chunk,),
        out_shape=(
            jax.ShapeDtypeStruct((FEAT, nodes), BF16),
            jax.ShapeDtypeStruct((FEAT, nodes), BF16),
        ),
        in_specs=[
            pl.BlockSpec((chunk, FEAT), lambda i: (i, 0)),
            pl.BlockSpec((FEAT, FEAT), lambda i: (0, 0)),
        ],
        out_specs=[
            pl.BlockSpec((FEAT, chunk), lambda i: (0, i)),
            pl.BlockSpec((FEAT, chunk), lambda i: (0, i)),
        ],
        compiler_params=params(),
        cost_estimate=pl.CostEstimate(
            flops=2 * nodes * FEAT * FEAT, bytes_accessed=12 * 10**6, transcendentals=nodes * FEAT
        ),
    )(agg_panel, weight_one_t)


def backward_kernel(
    table, tiles_hbm, hidden_hbm, slope_hbm, agg_hbm, weight_two, *rest
):
    pieces, rest = rest[:GZ], rest[GZ:]
    out, tiles, grads, total, hidden, slope, agg, sum_one, sum_two, sems = rest
    copies = [load_tiles(tiles_hbm, tiles, sems.at[0])]
    for d, piece in enumerate(pieces):
        for half in range(2):
            copy = pltpu.make_async_copy(
                piece.at[:, pl.ds(half * TB, TB)], grads.at[2 * d + half], sems.at[1]
            )
            copy.start()
            copies.append(copy)
    later = []
    for index, (held, place) in enumerate(((hidden_hbm, hidden), (slope_hbm, slope), (agg_hbm, agg))):
        copy = pltpu.make_async_copy(held, place, sems.at[index + 2])
        copy.start()
        later.append(copy)
    total[...] = jnp.zeros_like(total)
    for copy in copies:
        copy.wait()
    width = BWD_GROUPS * BWD

    def product(g):
        left, right = [], []
        for k in range(BWD):
            left.append(grads[table[width + g * BWD + k]])
            right.append(tiles[table[g * BWD + k]])
        return lax.dot_general(
            jnp.concatenate(left, 1),
            jnp.concatenate(right, 0),
            NN,
            preferred_element_type=F32,
        )

    def step(i, carry):
        first, second = product(2 * i), product(2 * i + 1)
        total[table[2 * width + 2 * i]] += first
        total[table[2 * width + 2 * i + 1]] += second
        return carry

    lax.fori_loop(0, (table[2 * width + BWD_GROUPS] + 1) // 2, step, 0)
    sum_one[...] = jnp.zeros_like(sum_one)
    sum_two[...] = jnp.zeros_like(sum_two)
    for copy in later:
        copy.wait()
    blocks = 8
    span = blocks * TB

    def finish(i, carry):
        back = jnp.concatenate([total[i * blocks + k] for k in range(blocks)], 1).astype(BF16)
        start = pl.multiple_of(i * span, span)
        grad = lax.dot_general(weight_two[...], back, NN, preferred_element_type=F32)
        grad = (grad * slope[:, pl.ds(start, span)].astype(F32)).astype(BF16)
        sum_one[...] += lax.dot_general(
            grad, agg[pl.ds(start, span), :], NN, preferred_element_type=F32
        )
        sum_two[...] += lax.dot_general(
            back, hidden[:, pl.ds(start, span)], NT, preferred_element_type=F32
        )
        return carry

    lax.fori_loop(0, 64 // blocks, finish, 0)
    out[0:FEAT] = sum_one[...].astype(BF16)
    out[FEAT : FEAT + CPAD] = sum_two[...].astype(BF16)
    out[FEAT + CPAD :] = jnp.zeros((512 - FEAT - CPAD, FEAT), BF16)


def backward(table, tiles, hidden_t, slope_t, agg_panel, weight_two, pieces):
    nodes = agg_panel.shape[0]
    return pl.pallas_call(
        backward_kernel,
        name="backward",
        out_shape=jax.ShapeDtypeStruct((512, FEAT), BF16),
        in_specs=[smem_spec()] + [any_spec()] * 4 + [vmem_spec()] + [any_spec()] * GZ,
        out_specs=vmem_spec(),
        scratch_shapes=[
            pltpu.VMEM((SLOTS + 1, TB, TB), BF16),
            pltpu.VMEM((16, CPAD, TB), BF16),
            pltpu.VMEM((64, CPAD, TB), F32),
            pltpu.VMEM((FEAT, nodes), BF16),
            pltpu.VMEM((FEAT, nodes), BF16),
            pltpu.VMEM((nodes, FEAT), BF16),
            pltpu.VMEM((FEAT, FEAT), F32),
            pltpu.VMEM((CPAD, FEAT), F32),
            pltpu.SemaphoreType.DMA((5,)),
        ],
        compiler_params=params(),
        cost_estimate=pl.CostEstimate(flops=5 * 10**9, bytes_accessed=2 * 10**7, transcendentals=0),
    )(table, tiles, hidden_t, slope_t, agg_panel, weight_two, *pieces)


def sum_everywhere(grads):
    shares = lax.all_to_all(grads.reshape(32, 16, FEAT), "row", 0, 0, tiled=True)
    share = jnp.sum(shares.astype(F32), 0).astype(BF16)
    shares = lax.all_to_all(
        jnp.broadcast_to(share, (GZ, 16, FEAT)), "col", 0, 0, tiled=True
    )
    share = jnp.sum(shares.astype(F32), 0).astype(BF16)
    full = lax.all_to_all(jnp.broadcast_to(share, (32, 16, FEAT)), "row", 0, 0, tiled=True)
    return full.reshape(512, FEAT)


def body(features, weight_one, weight_two, adj_tiles, tile_rows, tile_cols, tile_counts, labels):
    tiles = adj_tiles[0, 0]
    row_ids = tile_rows[0, 0]
    col_ids = tile_cols[0, 0]
    count = tile_counts[0, 0]
    z = lax.axis_index("col")
    node_total = ROWS * lax.axis_size("row") * lax.axis_size("col")
    weight_one_t = weight_one.T
    weight_two_pad = jnp.pad(weight_two, ((0, 0), (0, CPAD - CLASSES)))
    weight_two_t = weight_two_pad.T
    own_labels = lax.dynamic_slice_in_dim(labels, z * ROWS, ROWS, 0)[None, :]
    forward = group_tiles(row_ids, source_slots(col_ids), count, 16, FWD, FWD_GROUPS)
    row_slots = ((row_ids // 2 - z) % GZ) * 2 + row_ids % 2
    reverse = group_tiles(col_ids, row_slots, count, 64, BWD, BWD_GROUPS)

    parts = aggregate(forward, tiles, gather_row(features))
    parts = lax.all_to_all(parts, "col", 0, 0, tiled=True)
    agg, projected_t = middle(parts, weight_one, weight_two_t)
    agg_panel = lax.all_gather(agg, "row", axis=0, tiled=True)
    parts = partial_logits(forward, tiles, gather_row(projected_t))
    parts = lax.all_to_all(parts, "col", 0, 0, tiled=True)
    logits, grad_t = loss_grad(parts, own_labels, node_total ** (-0.5))
    grad_pieces = gather_col(grad_t)
    hidden_t, slope_t = gates(agg_panel, weight_one_t)
    grads = backward(reverse, tiles, hidden_t, slope_t, agg_panel, weight_two_pad, grad_pieces)
    grads = sum_everywhere(grads)
    grad_one = grads[:FEAT].astype(F32).T
    grad_two = grads[FEAT : FEAT + CLASSES].astype(F32).T
    return logits, grad_one, grad_two


def solution(mesh):
    in_specs = (
        P(("row", "col"), None),
        P(),
        P(),
        P("row", "col", None, None, None),
        P("row", "col", None),
        P("row", "col", None),
        P("row", "col"),
        P("row"),
    )
    out_specs = (P(("row", "col"), None), P(), P())
    return jax.shard_map(body, mesh=mesh, in_specs=in_specs, out_specs=out_specs, check_vma=False)
```

time: 800 us -> 252 us (0.32)
  waiting for transfers between devices: 540 us -> 72.9 us
  other arithmetic: 96.6 us -> 9.8 us
  local copies, waits for them, and re-layouts: 79.7 us -> 12.5 us
  starting transfers between devices: 0.24 us -> 66.2 us
  matrix products: 46.5 us -> 0 us
  Pallas kernels: 0 us -> 40.4 us
  blocking collectives: 20.4 us -> 34 us
    psum x1 -> x0, waiting for transfers between devices: 254 us -> none  [body(): grad_one = lax.psum(grad_one, ('row', 'col'))]
    reduce_scatter x3 -> x0, waiting for transfers between devices: 172 us -> none  [the longest x1 100 us: body(): lax.psum_scatter(partial_back, 'row', scatter_dimension=0, tiled=True)]
    all_gather x2 -> x1, waiting for transfers between devices: 114 us -> 0.01 us  [body(): agg_panel = lax.all_gather(agg, 'row', axis=0, tiled=True)]
    scatter-add x12 -> x0, other arithmetic: 82.2 us -> none  [one_group(): return running.at[target].add(product * live_mask[:, None, None])]
    all_to_all x0 -> x3, waiting for transfers between devices: none -> 56.8 us  [the longest x2 48.5 us: body(): parts = lax.all_to_all(parts, 'col', 0, 0, tiled=True)]
    ppermute x0 -> x29, starting transfers between devices: none -> 47.4 us  [the longest x22 38.5 us: gather_row(): send = lambda v, perm: lax.ppermute(v, 'row', perm)]
    gather x12 -> x0, local copies, waits for them, and re-layouts: 46.5 us -> none  [the longest x8 33.7 us: one_group(): picked = stacked[col_piece]]
    dot_general x16 -> x0, matrix products: 46.5 us -> none  [the longest x8 29.4 us: one_group(): jnp.einsum('gij,gjw->giw', tile_piece, picked, preferred_element_type=jnp...]
  transfers between devices with their start and end apart: 6 -> 33, of which waited for: 6 -> 11; matrix products, arithmetic and copies ran while one was open for 0% -> 6% of each run, Pallas kernels for 0% -> 7%
where the time goes in v1:
time: 252 us; the launch traced here: 251 us
  waiting for transfers between devices  72.9 us (29%)
  starting transfers between devices  66.2 us (26%)
  Pallas kernels  40.4 us (16%)
  blocking collectives  34 us (13%)
  between operations  15.2 us (6%)
  local copies, waits for them, and re-layouts  12.5 us (5%)
  other arithmetic  9.8 us (4%)
    all_to_all x2, waiting for transfers between devices, body(): parts = lax.all_to_all(parts, 'col', 0, 0, tiled=True)  48.5 us
    ppermute x22, starting transfers between devices, gather_row(): send = lambda v, perm: lax.ppermute(v, 'row', perm)  38.5 us
    all_to_all x1, blocking collectives, sum_everywhere(): lax.all_to_all(grads.reshape(32, 16, FEAT), 'row', 0, 0, tiled=True)  24 us
    all_to_all x2, starting transfers between devices, body(): parts = lax.all_to_all(parts, 'col', 0, 0, tiled=True)  13.5 us
    ppermute x22, waiting for transfers between devices, gather_row(): send = lambda v, perm: lax.ppermute(v, 'row', perm)  12.9 us
    pallas_call x1, Pallas kernels, backward(): pl.pallas_call(backward_kernel, name='backward', out_shape=jax.ShapeDtype...  12.6 us
    all_to_all x1, blocking collectives, sum_everywhere(): lax.all_to_all(jnp.broadcast_to(share, (GZ, 16, FEAT)), 'col', 0, 0, tile...  9.98 us
    pallas_call x1, Pallas kernels, gates(): pl.pallas_call(gates_kernel, name='gates', grid=(nodes // chunk,), out_sh...  9.18 us
  transfers between devices with their start and end apart: 33, of which 11 were waited for; matrix products, arithmetic and copies ran while one was open for 6% of the time, Pallas kernels for 7%

profile of v1, /device:TPU:1, one launch (start us, length us, event | category | flops | bytes accessed | tf_op | source)
XLA Modules:
  0.0 250.9 jit_solution(2534211713334861217)
XLA Ops:
  7.2 2.1 collective-permute-start.2
  9.3 2.5 collective-permute-start.1
  11.7 1.2 collective-permute-start
  16.0 0.9 constant_dynamic-update-slice_fusion.3
  17.2 2.8 %collective-permute-start.3 = (bf16[1024,256]{1,0:T(8,128)(2,1)S(1)}, bf16[1024,256]{1,0:T(8,128)(2,1)S(1)}, u32[]{:S(2)}, u32[]{:S(2)}) collective-permute-start(bf16[1024,256]{1,0:T(8,128)(2,1)S(1)} %constant_dynamic-update-slice_fusion), channel_id=1, source_target_pairs={{0,192},{8,56},{16,208},{24,8},{32,224},{40,24},{48,240},{56,40},{... | collective-permute-start | bytes 1572872 | tf_op jit(solution)/shard_map/ppermute | solution.py:66
  20.8 0.9 pad_maximum_fusion
  21.7 1.7 collective-permute-start.4
  23.5 5.4 %collective-permute-done.3 = bf16[1024,256]{1,0:T(8,128)(2,1)S(1)} collective-permute-done((bf16[1024,256]{1,0:T(8,128)(2,1)S(1)}, bf16[1024,256]{1,0:T(8,128)(2,1)S(1)}, u32[]{:S(2)}, u32[]{:S(2)}) %collective-permute-start.3) | collective-permute-done | bytes 524320 | tf_op jit(solution)/shard_map/ppermute | solution.py:66
  29.0 3.5 %collective-permute-start.5 = (bf16[512,256]{1,0:T(8,128)(2,1)S(1)}, bf16[512,256]{1,0:T(8,128)(2,1)S(1)}, u32[]{:S(2)}, u32[]{:S(2)}) collective-permute-start(bf16[512,256]{1,0:T(8,128)(2,1)S(1)} %slice.29), channel_id=1, source_target_pairs={{0,192},{8,56},{16,208},{24,8},{32,224},{40,24},{48,240},{56,40},{... | collective-permute-start | bytes 786440 | tf_op jit(solution)/shard_map/ppermute | solution.py:66
  32.5 2.6 %collective-permute-start.7 = (bf16[1024,256]{1,0:T(8,128)(2,1)S(1)}, bf16[1024,256]{1,0:T(8,128)(2,1)S(1)}, u32[]{:S(2)}, u32[]{:S(2)}) collective-permute-start(bf16[1024,256]{1,0:T(8,128)(2,1)S(1)} %constant_dynamic-update-slice_fusion), channel_id=1, source_target_pairs={{0,8},{8,0},{16,24},{24,16},{32,40},{40,32},{48,56},{56,48},{64,72... | collective-permute-start | bytes 1572872 | tf_op jit(solution)/shard_map/ppermute | solution.py:66
  35.8 3.2 %collective-permute-start.9 = (bf16[1024,256]{1,0:T(8,128)(2,1)S(1)}, bf16[1024,256]{1,0:T(8,128)(2,1)}, u32[]{:S(2)}, u32[]{:S(2)}) collective-permute-start(bf16[1024,256]{1,0:T(8,128)(2,1)S(1)} %constant_dynamic-update-slice_fusion.4), channel_id=1, source_target_pairs={{0,8},{8,0},{16,24},{24,16},{32,40},{40,32},{48,56},{56,48},{64,72... | collective-permute-start | bytes 1572872 | tf_op jit(solution)/shard_map/ppermute | solution.py:66
  39.1 0.8 select_reduce_fusion.5
  40.0 1.3 pad_add_fusion.table
  42.4 7.4 %aggregate.1 = bf16[8,256,256]{2,1,0:T(8,128)(2,1)} custom-call(s32[433]{0:T(512)} %pad_add_fusion.table, bf16[128,128,128]{2,1,0:T(8,128)(2,1)} %bitcast.42, bf16[8,128,256]{2,1,0:T(8,128)(2,1)} %bitcast.48, bf16[8,128,256]{2,1,0:T(8,128)(2,1)} %bitcast.45, bf16[8,128,256]{2,1,0:T(8,128)(2,1)} %bitcast.46, bf16[8,128,256]{2,1,0:T(8,128)(2,1)} %bitcast.52, ...), custom_call_target="tpu_custom_call" | custom-call | flops 2000000000 | bytes 10000000 | tf_op jit(solution)/shard_map/aggregate/pallas_call | solution.py:185
  49.7 9.7 %all-to-all-start = ((bf16[8,256,256]{2,1,0:T(8,128)(2,1)}), bf16[8,256,256]{2,1,0:T(8,128)(2,1)S(1)}, u32[]{:S(2)}, u32[]{:S(2)}) async-start(bf16[8,256,256]{2,1,0:T(8,128)(2,1)} %aggregate.1), calls=%async_computation | async-start | bytes 2097152 | tf_op jit(solution)/shard_map/all_to_all | solution.py:469
  61.0 27.7 %all-to-all-done.parts = bf16[8,256,256]{2,1,0:T(8,128)(2,1)S(1)} async-done(((bf16[8,256,256]{2,1,0:T(8,128)(2,1)}), bf16[8,256,256]{2,1,0:T(8,128)(2,1)S(1)}, u32[]{:S(2)}, u32[]{:S(2)}) %all-to-all-start) | async-done | bytes 1048608 | tf_op jit(solution)/shard_map/all_to_all | solution.py:469
  88.7 1.0 copy-done
  89.7 2.4 middle.1
  92.2 5.6 %collective-permute-start.12 = (bf16[176,256]{1,0:T(8,128)(2,1)}, bf16[176,256]{1,0:T(8,128)(2,1)S(1)}, u32[]{:S(2)}, u32[]{:S(2)}) collective-permute-start(bf16[176,256]{1,0:T(8,128)(2,1)} %get-tuple-element.9), channel_id=1, source_target_pairs={{0,32},{8,136},{16,48},{24,152},{32,0},{40,168},{48,16},{56,184},{... | collective-permute-start | bytes 270344 | tf_op jit(solution)/shard_map/ppermute | solution.py:66
  97.8 1.0 constant_dynamic-update-slice_fusion.9
  98.7 2.7 %collective-permute-done.11 = bf16[176,256]{1,0:T(8,128)(2,1)S(1)} collective-permute-done((bf16[176,256]{1,0:T(8,128)(2,1)}, bf16[176,256]{1,0:T(8,128)(2,1)S(1)}, u32[]{:S(2)}, u32[]{:S(2)}) %collective-permute-start.11) | collective-permute-done | bytes 90144 | tf_op jit(solution)/shard_map/ppermute | solution.py:66
  101.5 1.3 collective-permute-start.14
  103.2 0.9 pad_maximum_fusion.1
  104.1 1.3 collective-permute-start.15
  105.4 3.4 %collective-permute-done.14 = bf16[704,256]{1,0:T(8,128)(2,1)S(1)} collective-permute-done((bf16[704,256]{1,0:T(8,128)(2,1)S(1)}, bf16[704,256]{1,0:T(8,128)(2,1)S(1)}, u32[]{:S(2)}, u32[]{:S(2)}) %collective-permute-start.14) | collective-permute-done | bytes 360480 | tf_op jit(solution)/shard_map/ppermute | solution.py:66
  108.9 2.6 %collective-permute-start.16 = (bf16[352,256]{1,0:T(8,128)(2,1)S(1)}, bf16[352,256]{1,0:T(8,128)(2,1)S(1)}, u32[]{:S(2)}, u32[]{:S(2)}) collective-permute-start(bf16[352,256]{1,0:T(8,128)(2,1)S(1)} %slice.30), channel_id=1, source_target_pairs={{0,192},{8,56},{16,208},{24,8},{32,224},{40,24},{48,240},{56,40},{... | collective-permute-start | bytes 540680 | tf_op jit(solution)/shard_map/ppermute | solution.py:66
  111.5 4.0 %collective-permute-start.18 = (bf16[704,256]{1,0:T(8,128)(2,1)S(1)}, bf16[704,256]{1,0:T(8,128)(2,1)S(1)}, u32[]{:S(2)}, u32[]{:S(2)}) collective-permute-start(bf16[704,256]{1,0:T(8,128)(2,1)S(1)} %constant_dynamic-update-slice_fusion.6), channel_id=1, source_target_pairs={{0,8},{8,0},{16,24},{24,16},{32,40},{40,32},{48,56},{56,48},{64,72... | collective-permute-start | bytes 1081352 | tf_op jit(solution)/shard_map/ppermute | solution.py:66
  115.8 1.1 collective-permute-start.21
  116.9 1.7 collective-permute-start.20
  118.6 1.3 collective-permute-done.20
  120.6 6.8 %partial_logits.1 = bf16[8,176,256]{2,1,0:T(8,128)(2,1)} custom-call(s32[433]{0:T(512)} %pad_add_fusion.table, bf16[128,128,128]{2,1,0:T(8,128)(2,1)} %bitcast.43, bf16[4,176,256]{2,1,0:T(8,128)(2,1)} %bitcast.51, bf16[4,176,256]{2,1,0:T(8,128)(2,1)} %bitcast.49, bf16[4,176,256]{2,1,0:T(8,128)(2,1)} %bitcast.50, bf16[4,176,256]{2,1,0:T(8,128)(2,1)} %bitcast.56, ...), custom_call_target="tpu_custom_call" | custom-call | flops 2000000000 | bytes 10000000 | tf_op jit(solution)/shard_map/partial_logits/pallas_call | solution.py:272
  127.5 3.8 %all-to-all-start.1 = ((bf16[8,176,256]{2,1,0:T(8,128)(2,1)}), bf16[8,176,256]{2,1,0:T(8,128)(2,1)S(1)}, u32[]{:S(2)}, u32[]{:S(2)}) async-start(bf16[8,176,256]{2,1,0:T(8,128)(2,1)} %partial_logits.1), calls=%async_computation.1 | async-start | bytes 1441792 | tf_op jit(solution)/shard_map/all_to_all | solution.py:473
  131.2 1.3 dynamic_slice.3
  132.6 20.8 %all-to-all-done.1.parts = bf16[8,176,256]{2,1,0:T(8,128)(2,1)S(1)} async-done(((bf16[8,176,256]{2,1,0:T(8,128)(2,1)}), bf16[8,176,256]{2,1,0:T(8,128)(2,1)S(1)}, u32[]{:S(2)}, u32[]{:S(2)}) %all-to-all-start.1) | async-done | bytes 720928 | tf_op jit(solution)/shard_map/all_to_all | solution.py:473
  153.4 0.9 copy-done.1
  154.3 2.0 loss_grad.1
  156.5 1.5 collective-permute-start.26
  158.0 2.2 collective-permute-done.22.rest_1_
  160.2 1.5 collective-permute-start.23
  163.6 2.7 %collective-permute-start.24 = (bf16[176,256]{1,0:T(8,128)(2,1)S(1)}, bf16[176,256]{1,0:T(8,128)(2,1)S(1)}, u32[]{:S(2)}, u32[]{:S(2)}) collective-permute-start(bf16[176,256]{1,0:T(8,128)(2,1)S(1)} %collective-permute-done.23.rest_2_), channel_id=1, source_target_pairs={{0,7},{1,0},{2,1},{3,2},{4,3},{5,4},{6,5},{7,6},{8,15},{9,8},{10,9... | collective-permute-start | bytes 270344 | tf_op jit(solution)/shard_map/ppermute | solution.py:109
  166.3 1.4 pad_add_fusion.1.table
  167.9 3.0 %collective-permute-start.25 = (bf16[176,256]{1,0:T(8,128)(2,1)S(1)}, bf16[176,256]{1,0:T(8,128)(2,1)S(1)}, u32[]{:S(2)}, u32[]{:S(2)}) collective-permute-start(bf16[176,256]{1,0:T(8,128)(2,1)S(1)} %collective-permute-done.24.rest_3_), channel_id=1, source_target_pairs={{0,7},{1,0},{2,1},{3,2},{4,3},{5,4},{6,5},{7,6},{8,15},{9,8},{10,9... | collective-permute-start | bytes 270344 | tf_op jit(solution)/shard_map/ppermute | solution.py:109
  170.9 9.2 %gates.1 = (bf16[256,8192]{1,0:T(8,128)(2,1)}, bf16[256,8192]{1,0:T(8,128)(2,1)}) custom-call(bf16[8192,256]{1,0:T(8,128)(2,1)} %all-gather.2.cloned.1.call-done.agg.agg_hbm, bf16[256,256]{1,0:T(8,128)(2,1)} %bitcast.55), custom_call_target="tpu_custom_call" | custom-call | flops 1073741824 | bytes 12000000 | tf_op jit(solution)/shard_map/gates/pallas_call | solution.py:327
  180.8 12.6 %backward.1 = bf16[512,256]{1,0:T(8,128)(2,1)} custom-call(s32[491]{0:T(512)} %pad_add_fusion.1.table, bf16[128,128,128]{2,1,0:T(8,128)(2,1)} %bitcast.44, bf16[256,8192]{1,0:T(8,128)(2,1)} %get-tuple-element.12.hidden_hbm, bf16[256,8192]{1,0:T(8,128)(2,1)} %get-tuple-element.13.slope_hbm, bf16[8192,256]{1,0:T(8,128)(2,1)} %all-gather.2.cloned.1.call-done.agg.agg_hbm, ...), custom_call_target="tpu_custom_call" | custom-call | flops 5000000000 | bytes 20000000 | tf_op jit(solution)/shard_map/backward/pallas_call | solution.py:420
  193.4 24.0 %all_to_all.25 = bf16[32,16,256]{2,1,0:T(8,128)(2,1)S(1)} all-to-all(bf16[32,16,256]{2,1,0:T(8,128)(2,1)} %bitcast.61), channel_id=1, replica_groups=mesh['row'=32,'col'=8] {'row'}, dimensions={0} | all-to-all | bytes 524288 | tf_op jit(solution)/shard_map/all_to_all | solution.py:443
  217.5 10.0 %all_to_all.26 = bf16[8,16,256]{2,1,0:T(8,128)(2,1)S(1)} all-to-all(bf16[8,16,256]{2,1,0:T(8,128)(2,1)S(1)} %broadcast_in_dim.142), channel_id=1, replica_groups=mesh['row'=32,'col'=8] {'col'}, dimensions={0} | all-to-all | bytes 131072 | tf_op jit(solution)/shard_map/all_to_all | solution.py:445
  228.2 5.2 %all-to-all-start.4 = ((bf16[32,16,256]{2,1,0:T(8,128)(2,1)}), bf16[32,16,256]{2,1,0:T(8,128)(2,1)S(1)}, u32[]{:S(2)}, u32[]{:S(2)}) async-start(bf16[32,16,256]{2,1,0:T(8,128)(2,1)} %broadcast_in_dim.143), calls=%async_computation.4 | async-start | bytes 524288 | tf_op jit(solution)/shard_map/all_to_all | solution.py:449
  234.2 8.3 %all-to-all-done.4 = bf16[32,16,256]{2,1,0:T(8,128)(2,1)S(1)} async-done(((bf16[32,16,256]{2,1,0:T(8,128)(2,1)}), bf16[32,16,256]{2,1,0:T(8,128)(2,1)S(1)}, u32[]{:S(2)}, u32[]{:S(2)}) %all-to-all-start.4) | async-done | bytes 262176 | tf_op jit(solution)/shard_map/all_to_all | solution.py:449
  (131 shorter events, 14.5 us)
Async XLA Ops:
  7.2 10.0 %collective-permute-start.2 = (bf16[256,256]{1,0:T(8,128)(2,1)}, bf16[256,256]{1,0:T(8,128)(2,1)S(1)}, u32[]{:S(2)}, u32[]{:S(2)}) collective-permute-start(bf16[256,256]{1,0:T(8,128)(2,1)} %param.8), channel_id=1, source_target_pairs={{0,16},{8,72},{16,32},{24,88},{32,48},{40,104},{48,0},{56,120},{64... | collective-permute-start | bytes 393224 | tf_op jit(solution)/shard_map/ppermute | solution.py:66
  9.3 7.9 %collective-permute-start.1 = (bf16[256,256]{1,0:T(8,128)(2,1)}, bf16[256,256]{1,0:T(8,128)(2,1)S(1)}, u32[]{:S(2)}, u32[]{:S(2)}) collective-permute-start(bf16[256,256]{1,0:T(8,128)(2,1)} %param.8), channel_id=1, source_target_pairs={{0,32},{8,136},{16,48},{24,152},{32,0},{40,168},{48,16},{56,184},{... | collective-permute-start | bytes 393224 | tf_op jit(solution)/shard_map/ppermute | solution.py:66
  11.7 5.4 %collective-permute-start = (bf16[256,256]{1,0:T(8,128)(2,1)}, bf16[256,256]{1,0:T(8,128)(2,1)S(1)}, u32[]{:S(2)}, u32[]{:S(2)}) collective-permute-start(bf16[256,256]{1,0:T(8,128)(2,1)} %param.8), channel_id=1, source_target_pairs={{0,48},{8,200},{16,0},{24,216},{32,16},{40,232},{48,32},{56,248},{... | collective-permute-start | bytes 393224 | tf_op jit(solution)/shard_map/ppermute | solution.py:66
  17.2 24.2 %copy-start.4 = (bf16[1024,256]{1,0:T(8,128)(2,1)}, bf16[1024,256]{1,0:T(8,128)(2,1)S(1)}, u32[]{:S(2)}) copy-start(bf16[1024,256]{1,0:T(8,128)(2,1)S(1)} %constant_dynamic-update-slice_fusion) | copy-start | bytes 1572868
  17.2 11.7 %collective-permute-start.3 = (bf16[1024,256]{1,0:T(8,128)(2,1)S(1)}, bf16[1024,256]{1,0:T(8,128)(2,1)S(1)}, u32[]{:S(2)}, u32[]{:S(2)}) collective-permute-start(bf16[1024,256]{1,0:T(8,128)(2,1)S(1)} %constant_dynamic-update-slice_fusion), channel_id=1, source_target_pairs={{0,192},{8,56},{16,208},{24,8},{32,224},{40,24},{48,240},{56,40},{... | collective-permute-start | bytes 1572872 | tf_op jit(solution)/shard_map/ppermute | solution.py:66
  20.8 14.4 %collective-permute-start.6 = (bf16[1024,256]{1,0:T(8,128)(2,1)S(1)}, bf16[1024,256]{1,0:T(8,128)(2,1)S(1)}, u32[]{:S(2)}, u32[]{:S(2)}) collective-permute-start(bf16[1024,256]{1,0:T(8,128)(2,1)S(1)} %constant_dynamic-update-slice_fusion), channel_id=1, source_target_pairs={{0,64},{8,24},{16,80},{24,40},{32,96},{40,56},{48,112},{56,8},{64,... | collective-permute-start | bytes 1572872 | tf_op jit(solution)/shard_map/ppermute | solution.py:66
  21.7 13.3 %collective-permute-start.4 = (bf16[512,256]{1,0:T(8,128)(2,1)S(1)}, bf16[512,256]{1,0:T(8,128)(2,1)S(1)}, u32[]{:S(2)}, u32[]{:S(2)}) collective-permute-start(bf16[512,256]{1,0:T(8,128)(2,1)S(1)} %pad_maximum_fusion), channel_id=1, source_target_pairs={{0,128},{8,40},{16,144},{24,56},{32,160},{40,8},{48,176},{56,24},{... | collective-permute-start | bytes 786440 | tf_op jit(solution)/shard_map/ppermute | solution.py:66
  29.0 12.4 %copy-start.2 = (bf16[1024,256]{1,0:T(8,128)(2,1)}, bf16[1024,256]{1,0:T(8,128)(2,1)S(1)}, u32[]{:S(2)}) copy-start(bf16[1024,256]{1,0:T(8,128)(2,1)S(1)} %collective-permute-done.3) | copy-start | bytes 1572868
  29.0 6.8 %collective-permute-start.5 = (bf16[512,256]{1,0:T(8,128)(2,1)S(1)}, bf16[512,256]{1,0:T(8,128)(2,1)S(1)}, u32[]{:S(2)}, u32[]{:S(2)}) collective-permute-start(bf16[512,256]{1,0:T(8,128)(2,1)S(1)} %slice.29), channel_id=1, source_target_pairs={{0,192},{8,56},{16,208},{24,8},{32,224},{40,24},{48,240},{56,40},{... | collective-permute-start | bytes 786440 | tf_op jit(solution)/shard_map/ppermute | solution.py:66
  32.5 8.9 %collective-permute-start.7 = (bf16[1024,256]{1,0:T(8,128)(2,1)S(1)}, bf16[1024,256]{1,0:T(8,128)(2,1)S(1)}, u32[]{:S(2)}, u32[]{:S(2)}) collective-permute-start(bf16[1024,256]{1,0:T(8,128)(2,1)S(1)} %constant_dynamic-update-slice_fusion), channel_id=1, source_target_pairs={{0,8},{8,0},{16,24},{24,16},{32,40},{40,32},{48,56},{56,48},{64,72... | collective-permute-start | bytes 1572872 | tf_op jit(solution)/shard_map/ppermute | solution.py:66
  35.1 6.3 %collective-permute-start.8 = (bf16[1024,256]{1,0:T(8,128)(2,1)S(1)}, bf16[1024,256]{1,0:T(8,128)(2,1)S(1)}, u32[]{:S(2)}, u32[]{:S(2)}) collective-permute-start(bf16[1024,256]{1,0:T(8,128)(2,1)S(1)} %collective-permute-done.3), channel_id=1, source_target_pairs={{0,8},{8,0},{16,24},{24,16},{32,40},{40,32},{48,56},{56,48},{64,72... | collective-permute-start | bytes 1572872 | tf_op jit(solution)/shard_map/ppermute | solution.py:66
  35.2 6.2 %copy-start.8 = (bf16[1024,256]{1,0:T(8,128)(2,1)}, bf16[1024,256]{1,0:T(8,128)(2,1)S(1)}, u32[]{:S(2)}) copy-start(bf16[1024,256]{1,0:T(8,128)(2,1)S(1)} %collective-permute-done.6) | copy-start | bytes 1572868
  35.2 6.2 %collective-permute-start.10 = (bf16[1024,256]{1,0:T(8,128)(2,1)S(1)}, bf16[1024,256]{1,0:T(8,128)(2,1)}, u32[]{:S(2)}, u32[]{:S(2)}) collective-permute-start(bf16[1024,256]{1,0:T(8,128)(2,1)S(1)} %collective-permute-done.6), channel_id=1, source_target_pairs={{0,8},{8,0},{16,24},{24,16},{32,40},{40,32},{48,56},{56,48},{64,72... | collective-permute-start | bytes 1572872 | tf_op jit(solution)/shard_map/ppermute | solution.py:66
  35.8 5.6 %copy-start.3 = (bf16[1024,256]{1,0:T(8,128)(2,1)}, bf16[1024,256]{1,0:T(8,128)(2,1)S(1)}, u32[]{:S(2)}) copy-start(bf16[1024,256]{1,0:T(8,128)(2,1)S(1)} %constant_dynamic-update-slice_fusion.4) | copy-start | bytes 1572868
  35.8 5.6 %collective-permute-start.9 = (bf16[1024,256]{1,0:T(8,128)(2,1)S(1)}, bf16[1024,256]{1,0:T(8,128)(2,1)}, u32[]{:S(2)}, u32[]{:S(2)}) collective-permute-start(bf16[1024,256]{1,0:T(8,128)(2,1)S(1)} %constant_dynamic-update-slice_fusion.4), channel_id=1, source_target_pairs={{0,8},{8,0},{16,24},{24,16},{32,40},{40,32},{48,56},{56,48},{64,72... | collective-permute-start | bytes 1572872 | tf_op jit(solution)/shard_map/ppermute | solution.py:66
  42.4 17.1 %copy-start.18 = (bf16[256,172]{0,1:T(8,128)(2,1)S(1)}, bf16[256,172]{0,1:T(8,128)(2,1)}, u32[]{:S(2)}) copy-start(bf16[256,172]{0,1:T(8,128)(2,1)} %param.10) | copy-start | bytes 264196
  49.7 39.0 %all-to-all-start = ((bf16[8,256,256]{2,1,0:T(8,128)(2,1)}), bf16[8,256,256]{2,1,0:T(8,128)(2,1)S(1)}, u32[]{:S(2)}, u32[]{:S(2)}) async-start(bf16[8,256,256]{2,1,0:T(8,128)(2,1)} %aggregate.1), calls=%async_computation | async-start | bytes 2097152 | tf_op jit(solution)/shard_map/all_to_all | solution.py:469
  59.5 111.5 %all-gather.2.cloned.1.call-start = ((), (), s32[]{:S(2)}) async-start(), calls=%async_computation.5 | async-start | bytes 4325376 | tf_op jit(solution)/shard_map/all_gather | solution.py:471
  92.1 9.3 %collective-permute-start.13 = (bf16[176,256]{1,0:T(8,128)(2,1)}, bf16[176,256]{1,0:T(8,128)(2,1)S(1)}, u32[]{:S(2)}, u32[]{:S(2)}) collective-permute-start(bf16[176,256]{1,0:T(8,128)(2,1)} %get-tuple-element.9), channel_id=1, source_target_pairs={{0,16},{8,72},{16,32},{24,88},{32,48},{40,104},{48,0},{56,120},{64... | collective-permute-start | bytes 270344 | tf_op jit(solution)/shard_map/ppermute | solution.py:66
  92.2 9.2 %collective-permute-start.12 = (bf16[176,256]{1,0:T(8,128)(2,1)}, bf16[176,256]{1,0:T(8,128)(2,1)S(1)}, u32[]{:S(2)}, u32[]{:S(2)}) collective-permute-start(bf16[176,256]{1,0:T(8,128)(2,1)} %get-tuple-element.9), channel_id=1, source_target_pairs={{0,32},{8,136},{16,48},{24,152},{32,0},{40,168},{48,16},{56,184},{... | collective-permute-start | bytes 270344 | tf_op jit(solution)/shard_map/ppermute | solution.py:66
  97.8 3.6 %collective-permute-start.11 = (bf16[176,256]{1,0:T(8,128)(2,1)}, bf16[176,256]{1,0:T(8,128)(2,1)S(1)}, u32[]{:S(2)}, u32[]{:S(2)}) collective-permute-start(bf16[176,256]{1,0:T(8,128)(2,1)} %get-tuple-element.9), channel_id=1, source_target_pairs={{0,48},{8,200},{16,0},{24,216},{32,16},{40,232},{48,32},{56,248},{... | collective-permute-start | bytes 270344 | tf_op jit(solution)/shard_map/ppermute | solution.py:66
  101.5 18.4 %copy-start.7 = (bf16[704,256]{1,0:T(8,128)(2,1)}, bf16[704,256]{1,0:T(8,128)(2,1)S(1)}, u32[]{:S(2)}) copy-start(bf16[704,256]{1,0:T(8,128)(2,1)S(1)} %constant_dynamic-update-slice_fusion.6) | copy-start | bytes 1081348
  101.5 7.4 %collective-permute-start.14 = (bf16[704,256]{1,0:T(8,128)(2,1)S(1)}, bf16[704,256]{1,0:T(8,128)(2,1)S(1)}, u32[]{:S(2)}, u32[]{:S(2)}) collective-permute-start(bf16[704,256]{1,0:T(8,128)(2,1)S(1)} %constant_dynamic-update-slice_fusion.6), channel_id=1, source_target_pairs={{0,192},{8,56},{16,208},{24,8},{32,224},{40,24},{48,240},{56,40},{... | collective-permute-start | bytes 1081352 | tf_op jit(solution)/shard_map/ppermute | solution.py:66
  102.8 13.0 %collective-permute-start.17 = (bf16[704,256]{1,0:T(8,128)(2,1)S(1)}, bf16[704,256]{1,0:T(8,128)(2,1)S(1)}, u32[]{:S(2)}, u32[]{:S(2)}) collective-permute-start(bf16[704,256]{1,0:T(8,128)(2,1)S(1)} %constant_dynamic-update-slice_fusion.6), channel_id=1, source_target_pairs={{0,64},{8,24},{16,80},{24,40},{32,96},{40,56},{48,112},{56,8},{64,... | collective-permute-start | bytes 1081352 | tf_op jit(solution)/shard_map/ppermute | solution.py:66
  104.1 11.4 %collective-permute-start.15 = (bf16[352,256]{1,0:T(8,128)(2,1)S(1)}, bf16[352,256]{1,0:T(8,128)(2,1)S(1)}, u32[]{:S(2)}, u32[]{:S(2)}) collective-permute-start(bf16[352,256]{1,0:T(8,128)(2,1)S(1)} %pad_maximum_fusion.1), channel_id=1, source_target_pairs={{0,128},{8,40},{16,144},{24,56},{32,160},{40,8},{48,176},{56,24},{... | collective-permute-start | bytes 540680 | tf_op jit(solution)/shard_map/ppermute | solution.py:66
  108.9 11.0 %copy-start.5 = (bf16[704,256]{1,0:T(8,128)(2,1)}, bf16[704,256]{1,0:T(8,128)(2,1)S(1)}, u32[]{:S(2)}) copy-start(bf16[704,256]{1,0:T(8,128)(2,1)S(1)} %collective-permute-done.14) | copy-start | bytes 1081348
  108.9 8.0 %collective-permute-start.16 = (bf16[352,256]{1,0:T(8,128)(2,1)S(1)}, bf16[352,256]{1,0:T(8,128)(2,1)S(1)}, u32[]{:S(2)}, u32[]{:S(2)}) collective-permute-start(bf16[352,256]{1,0:T(8,128)(2,1)S(1)} %slice.30), channel_id=1, source_target_pairs={{0,192},{8,56},{16,208},{24,8},{32,224},{40,24},{48,240},{56,40},{... | collective-permute-start | bytes 540680 | tf_op jit(solution)/shard_map/ppermute | solution.py:66
  111.5 7.1 %collective-permute-start.18 = (bf16[704,256]{1,0:T(8,128)(2,1)S(1)}, bf16[704,256]{1,0:T(8,128)(2,1)S(1)}, u32[]{:S(2)}, u32[]{:S(2)}) collective-permute-start(bf16[704,256]{1,0:T(8,128)(2,1)S(1)} %constant_dynamic-update-slice_fusion.6), channel_id=1, source_target_pairs={{0,8},{8,0},{16,24},{24,16},{32,40},{40,32},{48,56},{56,48},{64,72... | collective-permute-start | bytes 1081352 | tf_op jit(solution)/shard_map/ppermute | solution.py:66
  115.5 3.1 %collective-permute-start.19 = (bf16[704,256]{1,0:T(8,128)(2,1)S(1)}, bf16[704,256]{1,0:T(8,128)(2,1)S(1)}, u32[]{:S(2)}, u32[]{:S(2)}) collective-permute-start(bf16[704,256]{1,0:T(8,128)(2,1)S(1)} %collective-permute-done.14), channel_id=1, source_target_pairs={{0,8},{8,0},{16,24},{24,16},{32,40},{40,32},{48,56},{56,48},{64,72... | collective-permute-start | bytes 1081352 | tf_op jit(solution)/shard_map/ppermute | solution.py:66
  115.8 2.8 %collective-permute-start.21 = (bf16[704,256]{1,0:T(8,128)(2,1)S(1)}, bf16[704,256]{1,0:T(8,128)(2,1)S(1)}, u32[]{:S(2)}, u32[]{:S(2)}) collective-permute-start(bf16[704,256]{1,0:T(8,128)(2,1)S(1)} %collective-permute-done.17), channel_id=1, source_target_pairs={{0,8},{8,0},{16,24},{24,16},{32,40},{40,32},{48,56},{56,48},{64,72... | collective-permute-start | bytes 1081352 | tf_op jit(solution)/shard_map/ppermute | solution.py:66
  116.9 3.0 %collective-permute-start.20 = (bf16[704,256]{1,0:T(8,128)(2,1)S(1)}, bf16[704,256]{1,0:T(8,128)(2,1)S(1)}, u32[]{:S(2)}, u32[]{:S(2)}) collective-permute-start(bf16[704,256]{1,0:T(8,128)(2,1)S(1)} %constant_dynamic-update-slice_fusion.10), channel_id=1, source_target_pairs={{0,8},{8,0},{16,24},{24,16},{32,40},{40,32},{48,56},{56,48},{64,72... | collective-permute-start | bytes 1081352 | tf_op jit(solution)/shard_map/ppermute | solution.py:66
  120.6 35.7 %copy-start.19 = (s32[1,1,128]{2,1,0:T(1,128)S(1)}, s32[1,1,128]{2,1,0:T(1,128)}, u32[]{:S(2)}) copy-start(s32[1,1,128]{2,1,0:T(1,128)} %param.13) | copy-start | bytes 1540
  120.6 41.2 %copy-start.11 = (bf16[256,256]{1,0:T(8,128)(2,1)S(1)}, bf16[256,256]{1,0:T(8,128)(2,1)}, u32[]{:S(2)}) copy-start(bf16[256,256]{1,0:T(8,128)(2,1)} %weight_one.1) | copy-start | bytes 393220
  127.5 26.0 %all-to-all-start.1 = ((bf16[8,176,256]{2,1,0:T(8,128)(2,1)}), bf16[8,176,256]{2,1,0:T(8,128)(2,1)S(1)}, u32[]{:S(2)}, u32[]{:S(2)}) async-start(bf16[8,176,256]{2,1,0:T(8,128)(2,1)} %partial_logits.1), calls=%async_computation.1 | async-start | bytes 1441792 | tf_op jit(solution)/shard_map/all_to_all | solution.py:473
  156.3 3.9 %collective-permute-start.22 = (bf16[176,256]{1,0:T(8,128)(2,1)}, bf16[176,256]{1,0:T(8,128)(2,1)S(1)}, u32[]{:S(2)}, u32[]{:S(2)}) collective-permute-start(bf16[176,256]{1,0:T(8,128)(2,1)} %get-tuple-element.14.rest_0_), channel_id=1, source_target_pairs={{0,7},{1,0},{2,1},{3,2},{4,3},{5,4},{6,5},{7,6},{8,15},{9,8},{10,9... | collective-permute-start | bytes 270344 | tf_op jit(solution)/shard_map/ppermute | solution.py:109
  156.5 6.2 %collective-permute-start.26 = (bf16[176,256]{1,0:T(8,128)(2,1)}, bf16[176,256]{1,0:T(8,128)(2,1)S(1)}, u32[]{:S(2)}, u32[]{:S(2)}) collective-permute-start(bf16[176,256]{1,0:T(8,128)(2,1)} %get-tuple-element.14.rest_0_), channel_id=1, source_target_pairs={{0,1},{1,2},{2,3},{3,4},{4,5},{5,6},{6,7},{7,0},{8,9},{9,10},{10,1... | collective-permute-start | bytes 270344 | tf_op jit(solution)/shard_map/ppermute | solution.py:109
  160.2 19.9 %copy-start.20 = (bf16[176,256]{1,0:T(8,128)(2,1)}, bf16[176,256]{1,0:T(8,128)(2,1)S(1)}, u32[]{:S(2)}) copy-start(bf16[176,256]{1,0:T(8,128)(2,1)S(1)} %collective-permute-done.22.rest_1_) | copy-start | bytes 270340
  160.2 3.4 %collective-permute-start.23 = (bf16[176,256]{1,0:T(8,128)(2,1)S(1)}, bf16[176,256]{1,0:T(8,128)(2,1)S(1)}, u32[]{:S(2)}, u32[]{:S(2)}) collective-permute-start(bf16[176,256]{1,0:T(8,128)(2,1)S(1)} %collective-permute-done.22.rest_1_), channel_id=1, source_target_pairs={{0,7},{1,0},{2,1},{3,2},{4,3},{5,4},{6,5},{7,6},{8,15},{9,8},{10,9... | collective-permute-start | bytes 270344 | tf_op jit(solution)/shard_map/ppermute | solution.py:109
  162.7 17.4 %copy-start.21 = (bf16[176,256]{1,0:T(8,128)(2,1)}, bf16[176,256]{1,0:T(8,128)(2,1)S(1)}, u32[]{:S(2)}) copy-start(bf16[176,256]{1,0:T(8,128)(2,1)S(1)} %collective-permute-done.26.rest_7_) | copy-start | bytes 270340
  162.7 5.0 %collective-permute-start.27 = (bf16[176,256]{1,0:T(8,128)(2,1)S(1)}, bf16[176,256]{1,0:T(8,128)(2,1)S(1)}, u32[]{:S(2)}, u32[]{:S(2)}) collective-permute-start(bf16[176,256]{1,0:T(8,128)(2,1)S(1)} %collective-permute-done.26.rest_7_), channel_id=1, source_target_pairs={{0,1},{1,2},{2,3},{3,4},{4,5},{5,6},{6,7},{7,0},{8,9},{9,10},{10,1... | collective-permute-start | bytes 270344 | tf_op jit(solution)/shard_map/ppermute | solution.py:109
  163.6 16.6 %copy-start.22 = (bf16[176,256]{1,0:T(8,128)(2,1)}, bf16[176,256]{1,0:T(8,128)(2,1)S(1)}, u32[]{:S(2)}) copy-start(bf16[176,256]{1,0:T(8,128)(2,1)S(1)} %collective-permute-done.23.rest_2_) | copy-start | bytes 270340
  163.6 4.3 %collective-permute-start.24 = (bf16[176,256]{1,0:T(8,128)(2,1)S(1)}, bf16[176,256]{1,0:T(8,128)(2,1)S(1)}, u32[]{:S(2)}, u32[]{:S(2)}) collective-permute-start(bf16[176,256]{1,0:T(8,128)(2,1)S(1)} %collective-permute-done.23.rest_2_), channel_id=1, source_target_pairs={{0,7},{1,0},{2,1},{3,2},{4,3},{5,4},{6,5},{7,6},{8,15},{9,8},{10,9... | collective-permute-start | bytes 270344 | tf_op jit(solution)/shard_map/ppermute | solution.py:109
  167.7 12.5 %copy-start.23 = (bf16[176,256]{1,0:T(8,128)(2,1)}, bf16[176,256]{1,0:T(8,128)(2,1)S(1)}, u32[]{:S(2)}) copy-start(bf16[176,256]{1,0:T(8,128)(2,1)S(1)} %collective-permute-done.27.rest_6_) | copy-start | bytes 270340
  167.7 12.4 %collective-permute-start.28 = (bf16[176,256]{1,0:T(8,128)(2,1)S(1)}, bf16[176,256]{1,0:T(8,128)(2,1)S(1)}, u32[]{:S(2)}, u32[]{:S(2)}) collective-permute-start(bf16[176,256]{1,0:T(8,128)(2,1)S(1)} %collective-permute-done.27.rest_6_), channel_id=1, source_target_pairs={{0,1},{1,2},{2,3},{3,4},{4,5},{5,6},{6,7},{7,0},{8,9},{9,10},{10,1... | collective-permute-start | bytes 270344 | tf_op jit(solution)/shard_map/ppermute | solution.py:109
  167.9 12.3 %copy-start.24 = (bf16[176,256]{1,0:T(8,128)(2,1)}, bf16[176,256]{1,0:T(8,128)(2,1)S(1)}, u32[]{:S(2)}) copy-start(bf16[176,256]{1,0:T(8,128)(2,1)S(1)} %collective-permute-done.24.rest_3_) | copy-start | bytes 270340
  167.9 12.2 %collective-permute-start.25 = (bf16[176,256]{1,0:T(8,128)(2,1)S(1)}, bf16[176,256]{1,0:T(8,128)(2,1)S(1)}, u32[]{:S(2)}, u32[]{:S(2)}) collective-permute-start(bf16[176,256]{1,0:T(8,128)(2,1)S(1)} %collective-permute-done.24.rest_3_), channel_id=1, source_target_pairs={{0,7},{1,0},{2,1},{3,2},{4,3},{5,4},{6,5},{7,6},{8,15},{9,8},{10,9... | collective-permute-start | bytes 270344 | tf_op jit(solution)/shard_map/ppermute | solution.py:109
  180.8 52.6 %copy-start.17 = (f32[256,172]{1,0:T(8,128)S(1)}, f32[256,172]{1,0:T(8,128)}, u32[]{:S(2)}) copy-start(f32[256,172]{1,0:T(8,128)} %get-tuple-element.21) | copy-start | bytes 528388
  228.2 14.3 %all-to-all-start.4 = ((bf16[32,16,256]{2,1,0:T(8,128)(2,1)}), bf16[32,16,256]{2,1,0:T(8,128)(2,1)S(1)}, u32[]{:S(2)}, u32[]{:S(2)}) async-start(bf16[32,16,256]{2,1,0:T(8,128)(2,1)} %broadcast_in_dim.143), calls=%async_computation.4 | async-start | bytes 524288 | tf_op jit(solution)/shard_map/all_to_all | solution.py:449
  (12 other events, 16.7 us)
Sparse Core Ops, SparseCore 0:
  92.2 49.7 all-gather.1
